TPU v7x, 128 devices: a whole 4x4x4 slice. The times are simulated.
128 devices in a mesh: sec: 2 (over z_lo), grp: 4 (over z_hi, core), shard: 16 (over x, y).
Axes of the slice: x: 4, y: 4, z: 4 (z_hi: 2, z_lo: 2; z = z_hi * 2 + z_lo), core: 2. Of those that a mesh axis runs over, the one named last changes fastest.
Arguments:
- queries: bfloat16 [512, 8192], P(('sec', 'grp', 'shard')), may hold values from -10 to 10
- cache_keys: bfloat16 [512, 512, 512], P(('sec', 'grp', 'shard')), may hold values from -10 to 10
- cache_values: bfloat16 [512, 512, 512], P(('sec', 'grp', 'shard')), may hold values from -6 to 6
- new_keys: bfloat16 [512, 512], P(('sec', 'grp', 'shard')), may hold values from -6 to 6
- new_values: bfloat16 [512, 512], P(('sec', 'grp', 'shard')), may hold values from -6 to 6
- lengths: int32 [512], P(('sec', 'grp', 'shard')), may hold values from 1 to 512, 131072 in all
- out_weight: bfloat16 [8192, 16384], P('shard', ('sec', 'grp')), may hold values from -0.5 to 0.5
- residual: bfloat16 [512, 16384], P('shard', ('sec', 'grp')), may hold values from -30 to 30
- norm_gain: float32 [16384], P(('sec', 'grp')), may hold values from 0.5 to 2
- gate_up: bfloat16 [16384, 2, 26624], P(('sec', 'grp'), None, 'shard'), may hold values from -0.046875 to 0.046875
- down_weight: bfloat16 [26624, 16384], P('shard', ('sec', 'grp')), may hold values from -0.078125 to 0.078125
Outputs:
- mixed: bfloat16 [512, 16384], P('shard', ('sec', 'grp'))
Inputs may be any that keep to these rules, and one draw needn't show every extreme that they name: Each row attends to its first lengths[r] cache slots and to its new token; some row has 512.
All inputs are finite; a program needn't handle non-finite values. No bound on the sum of `lengths` on one device may be relied on, other than what follows from the above.
Results may differ from a plain program's by a relative error of at most 0.011.
Values may be sent and summed in bfloat16 or wider, within the bound.
A program may use at most 128 MiB of HBM per device.

v0:
```python
import jax
import jax.numpy as jnp
from jax import lax
from jax.sharding import PartitionSpec as P

D = 16384
QH = 64
KVH = 4
HD = 128
LEN = 512


epsilon = 1e-05


def attend_rows(queries, cache_keys, cache_values, new_keys, new_values, lengths):
    rows_here = queries.shape[0]
    heads_per = QH // KVH
    scaling = HD ** (-0.5)
    query_heads = queries.reshape(rows_here, KVH, heads_per, HD)
    key_heads = cache_keys.reshape(rows_here, LEN, KVH, HD)
    value_heads = cache_values.reshape(rows_here, LEN, KVH, HD)
    scores = (
        jnp.einsum("rkgd,rlkd->rkgl", query_heads, key_heads, preferred_element_type=jnp.float32)
        * scaling
    )
    own_score = (
        jnp.einsum(
            "rkgd,rkd->rkg",
            query_heads,
            new_keys.reshape(rows_here, KVH, HD),
            preferred_element_type=jnp.float32,
        )
        * scaling
    )
    usable = lax.broadcasted_iota(jnp.int32, (rows_here, LEN), 1) < lengths[:, None]
    scores = jnp.where(usable[:, None, None, :], scores, -jnp.inf)
    highest = jnp.maximum(jnp.max(scores, axis=-1), own_score)
    weights = jnp.exp(scores - highest[..., None])
    own_weight = jnp.exp(own_score - highest)
    totals = jnp.sum(weights, axis=-1) + own_weight
    weights_low = weights.astype(jnp.bfloat16)
    own_low = own_weight.astype(jnp.bfloat16).astype(jnp.float32)
    numerator = jnp.einsum(
        "rkgl,rlkd->rkgd", weights_low, value_heads, preferred_element_type=jnp.float32
    )
    numerator = numerator + own_low[..., None] * new_values.astype(jnp.float32).reshape(
        rows_here, KVH, 1, HD
    )
    return (numerator / totals[..., None]).astype(jnp.bfloat16).reshape(rows_here, QH * HD)


def local(
    queries,
    cache_keys,
    cache_values,
    new_keys,
    new_values,
    lengths,
    out_weight,
    residual,
    norm_gain,
    gate_up,
    down_weight,
):
    attn = attend_rows(queries, cache_keys, cache_values, new_keys, new_values, lengths)
    head_block = lax.all_to_all(attn, "shard", split_axis=1, concat_axis=0, tiled=True)
    projected = jnp.dot(
        lax.all_gather(head_block, ("sec", "grp"), axis=0, tiled=True),
        out_weight,
        preferred_element_type=jnp.float32,
    )
    stream = residual.astype(jnp.float32) + lax.psum_scatter(
        projected, "shard", scatter_dimension=0, tiled=True
    )
    square_sum = lax.psum(jnp.sum(stream * stream, axis=1), ("sec", "grp"))
    normed = (stream * lax.rsqrt(square_sum / D + epsilon)[:, None] * norm_gain[None, :]).astype(
        jnp.bfloat16
    )
    both_weights = gate_up.reshape(gate_up.shape[0], -1)
    gate_and_up = jnp.dot(
        lax.all_gather(normed, "shard", axis=0, tiled=True),
        both_weights,
        preferred_element_type=jnp.float32,
    )
    hidden_width = down_weight.shape[0]
    summed = lax.psum(gate_and_up, ("sec", "grp"))
    hidden = (jax.nn.silu(summed[:, :hidden_width]) * summed[:, hidden_width:]).astype(jnp.bfloat16)
    partial_out = jnp.dot(hidden, down_weight, preferred_element_type=jnp.float32)
    feed_forward = lax.psum_scatter(partial_out, "shard", scatter_dimension=0, tiled=True)
    return (stream + feed_forward).astype(jnp.bfloat16)


def solution(mesh):
    placed = (
        P(("sec", "grp", "shard"), None),
        P(("sec", "grp", "shard"), None, None),
        P(("sec", "grp", "shard"), None, None),
        P(("sec", "grp", "shard"), None),
        P(("sec", "grp", "shard"), None),
        P(("sec", "grp", "shard")),
        P("shard", ("sec", "grp")),
        P("shard", ("sec", "grp")),
        P(("sec", "grp")),
        P(("sec", "grp"), None, "shard"),
        P("shard", ("sec", "grp")),
    )
    return jax.shard_map(
        local, mesh=mesh, in_specs=placed, out_specs=P("shard", ("sec", "grp")), check_vma=False
    )
```

profile of v0, /device:TPU:1, one launch (start us, length us, event | category | flops | bytes accessed | tf_op | source)
XLA Modules:
  0.0 380.0 jit_solution(13203357584083665862)
XLA Ops:
  6.5 0.9 iota_compare_fusion
  7.4 0.7 reshape.51
  8.1 0.7 reshape.47
  8.8 1.0 copy.21
  9.8 0.1 fusion.32
  10.0 2.3 fusion.31
  12.3 0.2 fusion.25
  12.6 0.5 fusion.22
  13.0 0.1 all_to_all.14
  13.1 0.1 copy.16
  13.2 13.9 %all_to_all.19 = bf16[4,16,512]{2,0,1:T(4,128)(2,1)S(1)} all-to-all(bf16[4,16,512]{2,0,1:T(4,128)(2,1)S(1)} %copy.16), channel_id=1, replica_groups=mesh['sec'=2,'grp'=4,'shard'=16] {'shard'}, dimensions={1} | all-to-all | bytes 131072 | tf_op jit(solution)/shard_map/all_to_all | solution.py:67
  27.1 17.4 %all_gather.6 = bf16[512,512]{1,0:T(8,128)(2,1)S(1)} all-gather(bf16[64,512]{1,0:T(8,128)(2,1)S(1)} %all_to_all.17), channel_id=1, replica_groups=mesh['sec'=2,'grp'=4,'shard'=16] {'sec','grp'}, dimensions={0}, use_global_device_ids=true | all-gather | bytes 589824 | tf_op jit(solution)/shard_map/all_gather | solution.py:69
  44.5 3.2 fusion.33
  47.8 73.5 %reduce-scatter.3.cloned.1.call-done = f32[32,2048]{1,0:T(8,128)} async-done(((f32[512,2048]{1,0:T(8,128)}), f32[32,2048]{1,0:T(8,128)}) %reduce-scatter.3.cloned.1.call-update) | async-done | bytes 262160 | tf_op jit(solution)/shard_map/reduce_scatter | solution.py:73
  121.2 1.1 multiply_reduce_fusion
  122.3 14.3 %psum.14 = f32[32]{0:T(128)S(1)} all-reduce(f32[32]{0:T(128)S(1)} %multiply_reduce_fusion), channel_id=1, replica_groups=mesh['sec'=2,'grp'=4,'shard'=16] {'sec','grp'}, use_global_device_ids=true, to_apply=%region_4.5 | all-reduce | flops 32 | bytes 256 | tf_op jit(solution)/shard_map/psum | solution.py:76
  136.7 1.7 multiply_convert_fusion
  138.4 14.3 %copy.22 = bf16[256,8,2,1664]{3,1,2,0:T(8,128)(2,1)} copy(bf16[256,8,2,1664]{3,2,1,0:T(2,128)(2,1)} %bitcast.44) | data formatting | bytes 27262976
  152.7 29.5 %all-gather.2.cloned.1.call-done = bf16[512,2048]{1,0:T(8,128)(2,1)} async-done(((bf16[32,2048]{1,0:T(8,128)(2,1)}), bf16[512,2048]{1,0:T(8,128)(2,1)}) %all-gather.2.cloned.1.call-update) | async-done | bytes 2097168 | tf_op jit(solution)/shard_map/all_gather | solution.py:82
  182.2 13.2 %fusion.34 = f32[512,3328]{1,0:T(8,128)} fusion(bf16[512,2048]{1,0:T(8,128)(2,1)} %all-gather.2.cloned.1.call-done, bf16[2048,3328]{1,0:T(8,128)(2,1)} %bitcast.45), kind=kOutput, calls=%fused_computation.33 | convolution fusion | flops 6979321856 | bytes 22544384 | tf_op jit(solution)/shard_map/dot_general | solution.py:81
  195.5 89.1 %all-reduce.2.cloned.1.call-done = f32[512,3328]{1,0:T(8,128)} async-done(((f32[512,3328]{1,0:T(8,128)}), f32[512,3328]{1,0:T(8,128)}) %all-reduce.2.cloned.1.call-update) | async-done | bytes 6815760 | tf_op jit(solution)/shard_map/psum | solution.py:87
  284.7 11.0 %fusion.7 = f32[512,2048]{1,0:T(8,128)} fusion(bf16[1664,2048]{1,0:T(8,128)(2,1)} %param.21, f32[512,3328]{1,0:T(8,128)} %all-reduce.2.cloned.1.call-done), kind=kOutput, calls=%fused_computation.8 | convolution fusion | flops 3494772736 | bytes 17825792 | tf_op jit(solution)/shard_map/dot_general | solution.py:89
  295.7 76.1 %reduce-scatter.5.cloned.1.call-done = f32[32,2048]{1,0:T(8,128)} async-done(((f32[512,2048]{1,0:T(8,128)}), f32[32,2048]{1,0:T(8,128)}) %reduce-scatter.5.cloned.1.call-update) | async-done | bytes 262160 | tf_op jit(solution)/shard_map/reduce_scatter | solution.py:90
  371.8 1.6 add_convert_fusion
  (22 shorter events, 0.3 us)
Async XLA Ops:
  6.5 38.0 %copy-start = (bf16[512,2048]{1,0:T(8,128)(2,1)S(1)}, bf16[512,2048]{1,0:T(8,128)(2,1)}, u32[]{:S(2)}) copy-start(bf16[512,2048]{1,0:T(8,128)(2,1)} %param.17) | copy-start | bytes 6291460
  6.5 114.7 %reduce-scatter.3.cloned.1.call-start = ((), (), s32[]{:S(2)}) async-start(), calls=%async_computation.3 | async-start | bytes 4456448 | tf_op jit(solution)/shard_map/reduce_scatter | solution.py:73
  8.8 3.8 copy-start.4
  47.7 73.5 %copy-start.2 = (bf16[32,2048]{1,0:T(8,128)(2,1)S(1)}, bf16[32,2048]{1,0:T(8,128)(2,1)}, u32[]{:S(2)}) copy-start(bf16[32,2048]{1,0:T(8,128)(2,1)} %param.18) | copy-start | bytes 393220
  47.7 89.0 %copy-start.3 = (f32[2048]{0:T(1024)S(1)}, f32[2048]{0:T(1024)}, u32[]{:S(2)}) copy-start(f32[2048]{0:T(1024)} %param.19) | copy-start | bytes 24580
  47.7 134.5 %all-gather.2.cloned.1.call-start = ((), (), s32[]{:S(2)}) async-start(), calls=%async_computation.4 | async-start | bytes 2228224 | tf_op jit(solution)/shard_map/all_gather | solution.py:82
  138.4 146.3 %all-reduce.2.cloned.1.call-start = ((), (), s32[]{:S(2)}) async-start(), calls=%async_computation.5 | async-start | bytes 13631488 | tf_op jit(solution)/shard_map/psum | solution.py:87
  195.5 176.3 %reduce-scatter.5.cloned.1.call-start = ((), (), s32[]{:S(2)}) async-start(), calls=%async_computation.6 | async-start | bytes 4456448 | tf_op jit(solution)/shard_map/reduce_scatter | solution.py:90
  295.7 76.1 %copy-start.1 = (f32[32,2048]{1,0:T(8,128)S(1)}, f32[32,2048]{1,0:T(8,128)}, u32[]{:S(2)}) copy-start(f32[32,2048]{1,0:T(8,128)} %reduce-scatter.3.cloned.1.call-done) | copy-start | bytes 786436
Sparse Core Ops, SparseCore 0:
  47.9 73.3 reduce-scatter.2
  138.5 43.6 all-gather.1
  195.6 89.0 all-reduce.1
  295.8 75.9 reduce-scatter.4
where the time goes:
time: 381 us; the launch traced here: 380 us
  waiting for transfers between devices  268 us (70%)
  blocking collectives  45.6 us (12%)
  matrix products  30.4 us (8%)
  local copies, waits for them, and re-layouts  16.8 us (4%)
  between operations  13.2 us (3%)
  other arithmetic  5.59 us (1%)
    psum x1, waiting for transfers between devices, local(): summed = lax.psum(gate_and_up, ('sec', 'grp'))  89.1 us
    reduce_scatter x1, waiting for transfers between devices, local(): lax.psum_scatter(partial_out, 'shard', scatter_dimension=0, tiled=True)  76.1 us
    reduce_scatter x1, waiting for transfers between devices, local(): lax.psum_scatter(projected, 'shard', scatter_dimension=0, tiled=True)  73.5 us
    all_gather x1, waiting for transfers between devices, local(): lax.all_gather(normed, 'shard', axis=0, tiled=True)  29.5 us
    all_gather x1, blocking collectives, local(): lax.all_gather(head_block, ('sec', 'grp'), axis=0, tiled=True)  17.4 us
    unnamed x12, local copies, waits for them, and re-layouts  15.3 us
    psum x1, blocking collectives, local(): square_sum = lax.psum(jnp.sum(stream * stream, axis=1), ('sec', 'grp'))  14.3 us
    all_to_all x1, blocking collectives, local(): lax.all_to_all(attn, 'shard', split_axis=1, concat_axis=0, tiled=True)  13.9 us
  transfers between devices with their start and end apart: 4, of which 4 were waited for; matrix products, arithmetic and copies ran while one was open for 4% of the time, Pallas kernels for 0%

commit v1 on v0

v1 whole, which is shorter than its diff:
```python
import jax
import jax.numpy as jnp
from jax import lax
from jax.experimental import pallas as pl
from jax.experimental.pallas import tpu as pltpu
from jax.sharding import PartitionSpec as P

MESH = pl.DeviceIdType.MESH
BF = jnp.bfloat16
F32 = jnp.float32

D = 16384
KVH = 4
HD = 128
LEN = 512
ROWS = 512
FEATURES = 2048
HIDDEN = 1664
EPSILON = 1e-05

CHUNKS = 2
R = 32 // CHUNKS
HALF = FEATURES // 2
TILE = 256
FIRST = 7 * TILE
PIECES = 4
LAG = 0

HALVES = (slice(0, HALF), slice(HALF, FEATURES))
GROUPS = (slice(0, FIRST), slice(FIRST, 2 * HIDDEN))


def kernel(
    lengths, queries, new_keys, new_values, residual, norm_gain,
    cache_keys, cache_values, out_weight, gate_up, down_weight,
    mixed,
    keys, values, wo, raw, gu, wd, q_rows, att, tiles, arrived, attn, unweave, regroup,
    part, part_in, slab, slab_in, rows, stream, squares, squares_in,
    gates, gates_core, gates_in, hidden,
    send_sem, recv_sem, local_sem,
):
    sec = lax.axis_index("sec")
    grp = lax.axis_index("grp")
    shard = lax.axis_index("shard")
    z = (grp // 2) * 2 + sec
    core = grp % 2
    x = shard // 4
    y = shard % 4
    block = sec * 4 + grp

    def plane(at):
        return {"shard": at}

    def along_x(d):
        return {"shard": ((x + d) % 4) * 4 + y}

    def along_y(d):
        return {"shard": x * 4 + (y + d) % 4}

    def along_z(d, other=False):
        to = (z + d) % 4
        c = 1 - core if other else core
        return {"sec": to % 2, "grp": (to // 2) * 2 + c}

    def across():
        return {"grp": (grp // 2) * 2 + (1 - core)}

    sent = []

    def send(src, dst, to):
        i = len(sent)
        copy = pltpu.make_async_remote_copy(
            src_ref=src, dst_ref=dst, send_sem=send_sem.at[i], recv_sem=recv_sem.at[i],
            device_id=to, device_id_type=MESH,
        )
        copy.start()
        sent.append(copy)
        return copy

    fetched = []

    def fetch(src, dst):
        copy = pltpu.make_async_copy(src, dst, local_sem.at[len(fetched)])
        copy.start()
        fetched.append(copy)
        return copy

    cache = [
        (fetch(cache_keys.at[r], keys.at[r]), fetch(cache_values.at[r], values.at[r]))
        for r in range(4)
    ]
    barrier = pltpu.get_barrier_semaphore()
    for d in range(1, 16):
        pl.semaphore_signal(barrier, inc=1, device_id=plane((shard + d) % 16), device_id_type=MESH)
    for d in range(1, 4):
        pl.semaphore_signal(barrier, inc=1, device_id=along_z(d), device_id_type=MESH)
        pl.semaphore_signal(barrier, inc=1, device_id=along_z(d, True), device_id_type=MESH)
    pl.semaphore_signal(barrier, inc=1, device_id=across(), device_id_type=MESH)

    wo_in = fetch(out_weight, wo)
    woven = gate_up.reshape(2 * FEATURES, HIDDEN)
    depth = 2 * FEATURES // PIECES

    def fetch_raw(p):
        return fetch(woven.at[pl.ds(p * depth, depth), :], raw.at[p % 2])

    raw_in = {0: fetch_raw(0), 1: fetch_raw(1)}
    wd_in = fetch(down_weight, wd)

    i = lax.broadcasted_iota(jnp.int32, (256, 256), 0)
    j = lax.broadcasted_iota(jnp.int32, (256, 256), 1)
    unweave[...] = jnp.where(j == (i % 128) * 2 + i // 128, 1.0, 0.0).astype(BF)
    regroup[...] = jnp.where(
        j == ((i % 64) // 4) * 16 + (i % 4) * 4 + i // 64, 1.0, 0.0
    ).astype(BF)

    def unweave_piece(p):
        raw_in[p].wait()

        def body(step, carry):
            at = pl.multiple_of(step * 256, 256)
            both = jnp.dot(
                unweave[...], raw[p % 2, pl.ds(at, 256), :], preferred_element_type=F32
            ).astype(BF)
            to = pl.ds(pl.multiple_of(p * (depth // 2) + step * 128, 128), 128)
            gu[to, 0:HIDDEN] = both[:128]
            gu[to, HIDDEN:] = both[128:]
            return carry

        lax.fori_loop(0, depth // 256, body, 0)
        if p + 2 < PIECES:
            raw_in[p + 2] = fetch_raw(p + 2)

    scaling = HD ** (-0.5)
    for h in range(KVH * 16):
        q_rows[:, h, :] = queries[:, h * HD:(h + 1) * HD].astype(F32)
    own_keys = new_keys[...].astype(F32)
    own_values = new_values[...].astype(F32)
    slots = lax.broadcasted_iota(jnp.int32, (1, LEN), 1)
    for r in range(4):
        cache[r][0].wait()
        cache[r][1].wait()
        usable = slots < lengths[r]
        for k in range(KVH):
            of_head = slice(k * HD, (k + 1) * HD)
            query = q_rows[r, k * 16:(k + 1) * 16, :]
            scores = lax.dot_general(
                query.astype(BF), keys[r, :, of_head], (((1,), (1,)), ((), ())),
                preferred_element_type=F32,
            ) * scaling
            own = jnp.sum(query * own_keys[r:r + 1, of_head], axis=1, keepdims=True) * scaling
            scores = jnp.where(usable, scores, -1e30)
            top = jnp.maximum(jnp.max(scores, axis=1, keepdims=True), own)
            weights = jnp.exp(scores - top)
            own_weight = jnp.exp(own - top)
            total = jnp.sum(weights, axis=1, keepdims=True) + own_weight
            summed = jnp.dot(
                weights.astype(BF), values[r, :, of_head], preferred_element_type=F32
            ) + own_weight.astype(BF).astype(F32) * own_values[r:r + 1, of_head]
            result = summed / total
            for g in range(4):
                att[4 * k + g, 4 * r:4 * r + 4, :] = result[4 * g:4 * g + 4, :]
    tiles[...] = att[...].astype(BF)

    pl.semaphore_wait(barrier, 22)

    exchange = []
    for d in range(1, 16):
        to = (shard + d) % 16
        exchange.append(send(tiles.at[to], arrived.at[shard], plane(to)))
    arrived[shard] = tiles[shard]
    unweave_piece(0)
    for copy in exchange:
        copy.wait_recv()
    grouped = jnp.dot(
        regroup[...], arrived[...].reshape(256, HD), preferred_element_type=F32
    ).astype(BF)
    for h in range(4):
        of_head = grouped[h * 64:(h + 1) * 64, :].reshape(2, CHUNKS, R, HD)
        for c in range(CHUNKS):
            attn[c, pl.ds(2 * block, 2), :, h * HD:(h + 1) * HD] = of_head[:, c]
    gather = []
    mine = attn.at[:, pl.ds(2 * block, 2)]
    for d in (2, 1, 3):
        gather.append(send(mine, mine, along_z(d)))
        gather.append(send(mine, mine, along_z(d, True)))
    gather.append(send(mine, mine, across()))
    unweave_piece(1)
    wo_in.wait()
    for copy in gather:
        copy.wait_recv()

    gain = norm_gain[...].reshape(1, FEATURES)
    unscale = 1.0 / (gain * gain)

    def product(c, lhs, weight, half, dst):
        start = half.start
        count = (half.stop - start) // TILE

        def body(step, carry):
            at = pl.ds(pl.multiple_of(start + step * TILE, TILE), TILE)
            tile = jnp.dot(
                lhs[...].reshape(16 * R, lhs.shape[-1]), weight[:, at],
                preferred_element_type=F32,
            ).astype(BF)
            dst[c, :, :, at] = tile.reshape(16, R, TILE)
            return carry

        lax.fori_loop(0, count, body, 0)

    def scatter_out(u, c, h):
        copies = []
        grid = part.at[u, c].reshape(4, 4, R, FEATURES)
        for n, d in enumerate((2, 1, 3)):
            if h == 0:
                src, to = grid.at[(x + d) % 4, :, :, HALVES[h]], along_x(d)
            else:
                src, to = grid.at[:, (y + d) % 4, :, HALVES[h]], along_y(d)
            copies.append(send(src, part_in.at[u, c, h, n], to))
        return copies

    def scatter_mid(u, c, h, copies):
        for copy in copies:
            copy.wait_recv()
        grid = part.at[u, c].reshape(4, 4, R, FEATURES)
        total = (grid[x, :, :, HALVES[h]] if h == 0 else grid[:, y, :, HALVES[h]]).astype(F32)
        for n in range(3):
            total = total + part_in[u, c, h, n].astype(F32)
        slab[u, c, h] = total.astype(BF)
        out = []
        for n, d in enumerate((2, 1, 3)):
            if h == 0:
                src, to = slab.at[u, c, h, (y + d) % 4], along_y(d)
            else:
                src, to = slab.at[u, c, h, (x + d) % 4], along_x(d)
            out.append(send(src, slab_in.at[u, c, h, n], to))
        return out

    def scatter_end(u, c, h, copies):
        for copy in copies:
            copy.wait_recv()
        total = slab[u, c, h, y if h == 0 else x].astype(F32)
        for n in range(3):
            total = total + slab_in[u, c, h, n].astype(F32)
        return total

    def chain(c):
        lhs = attn.at[c]
        first = []
        for h in (0, 1):
            product(c, lhs, wo, HALVES[h], part.at[0])
            first.append(scatter_out(0, c, h))
            yield
        second = []
        for h in (0, 1):
            second.append(scatter_mid(0, c, h, first[h]))
            yield
        gathers = []
        for h in (0, 1):
            cols = HALVES[h]
            value = residual[c * R:(c + 1) * R, cols].astype(F32) + scatter_end(0, c, h, second[h])
            stream[c, :, cols] = value
            rows[c, x, y, :, cols] = (value * gain[:, cols]).astype(BF)
            here = rows.at[c, x, y, :, cols]
            gathers.append([
                send(here, here, along_y(d) if h == 0 else along_x(d)) for d in (2, 1, 3)
            ])
        yield
        wider = []
        for h in (0, 1):
            for copy in gathers[h]:
                copy.wait_recv()
            here = rows.at[c, x, :, :, HALVES[h]] if h == 0 else rows.at[c, :, y, :, HALVES[h]]
            wider += [send(here, here, along_x(d) if h == 0 else along_y(d)) for d in (2, 1, 3)]
            yield
        for copy in wider:
            copy.wait_recv()

        def square(b, carry):
            v = rows[c, b // 4, b % 4].astype(F32)
            total = jnp.sum(v * v * unscale, axis=1, keepdims=True)
            squares[c, b] = jnp.broadcast_to(total, (R, 128))
            return carry

        lax.fori_loop(0, 16, square, 0)
        square_copies = []
        n = 0
        for other in (False, True):
            for d in (0, 1, 2, 3):
                if d == 0 and not other:
                    continue
                owner = (1 - core if other else core) * 4 + (z + d) % 4
                square_copies.append(send(
                    squares.at[c, pl.ds(2 * owner, 2)], squares_in.at[c, n],
                    across() if d == 0 else along_z(d, other),
                ))
                n += 1
        yield
        lhs = rows.at[c].reshape(16, R, FEATURES)
        crossing = []
        theirs = pl.ds(8 * (1 - core), 8)
        for g in (0, 1):
            product(c, lhs, gu, GROUPS[g], gates)
            crossing.append(send(
                gates.at[c, theirs, :, GROUPS[g]], gates_core.at[c, :, :, GROUPS[g]], across()
            ))
            yield
        reduced = []
        for g in (0, 1):
            crossing[g].wait_recv()
            for n, d in enumerate((2, 1, 3)):
                to = (z + d) % 4
                at = pl.ds(8 * core + 2 * to, 2)
                gates[c, at, :, GROUPS[g]] = (
                    gates[c, at, :, GROUPS[g]].astype(F32)
                    + gates_core[c, pl.ds(2 * to, 2), :, GROUPS[g]].astype(F32)
                ).astype(BF)
                reduced.append(send(
                    gates.at[c, at, :, GROUPS[g]], gates_in.at[c, n, :, :, GROUPS[g]], along_z(d)
                ))
            yield
        for copy in square_copies + reduced:
            copy.wait_recv()
        owner = 2 * (4 * core + z)
        total = squares[c, pl.ds(owner, 2)]
        for n in range(7):
            total = total + squares_in[c, n]
        scale = lax.rsqrt(total / D + EPSILON)[:, :, 0:1]

        def summed(cols):
            total = gates[c, pl.ds(owner, 2), :, cols].astype(F32)
            total = total + gates_core[c, pl.ds(2 * z, 2), :, cols].astype(F32)
            for n in range(3):
                total = total + gates_in[c, n, :, :, cols].astype(F32)
            return total * scale

        gate = summed(slice(0, HIDDEN))
        up = summed(slice(HIDDEN, 2 * HIDDEN))
        hidden[c, pl.ds(owner, 2)] = (gate / (1.0 + jnp.exp(-gate)) * up).astype(BF)
        here = hidden.at[c, pl.ds(owner, 2)]
        spread = [send(here, here, along_z(d)) for d in (2, 1, 3)]
        over = [send(here, here, across())]
        yield
        for d, copy in sorted(zip((2, 1, 3), spread), key=lambda e: e[0] == 2):
            copy.wait_recv()
            there = hidden.at[c, pl.ds(2 * (4 * core + (z - d + 4) % 4), 2)]
            over.append(send(there, there, across()))
        yield
        for copy in over:
            copy.wait_recv()
        lhs = hidden.at[c]
        first = []
        for h in (0, 1):
            product(c, lhs, wd, HALVES[h], part.at[1])
            first.append(scatter_out(1, c, h))
            yield
        second = []
        for h in (0, 1):
            second.append(scatter_mid(1, c, h, first[h]))
            yield
        for h in (0, 1):
            cols = HALVES[h]
            mixed[c * R:(c + 1) * R, cols] = (
                stream[c, :, cols] + scatter_end(1, c, h, second[h])
            ).astype(BF)

    chains = [chain(c) for c in range(CHUNKS)]
    done = [0] * CHUNKS
    live = [True] * CHUNKS
    rest = [lambda: unweave_piece(2), lambda: unweave_piece(3)]

    def advance(c):
        if live[c]:
            try:
                next(chains[c])
                done[c] += 1
            except StopIteration:
                live[c] = False

    turn = 0
    while any(live):
        for c in range(CHUNKS):
            if turn >= c * LAG:
                advance(c)
        turn += 1
        if turn == 2:
            for piece in rest:
                piece()
            wd_in.wait()
    for copy in sent:
        copy.wait_send()


SENDS = 15 + 7 + CHUNKS * (6 + 6 + 6 + 6 + 7 + 2 + 6 + 3 + 4 + 6 + 6)


def local(
    queries, cache_keys, cache_values, new_keys, new_values, lengths,
    out_weight, residual, norm_gain, gate_up, down_weight,
):
    vmem = pl.BlockSpec(memory_space=pltpu.VMEM)
    smem = pl.BlockSpec(memory_space=pltpu.SMEM)
    anywhere = pl.BlockSpec(memory_space=pl.ANY)
    return pl.pallas_call(
        kernel,
        out_shape=jax.ShapeDtypeStruct((32, FEATURES), BF),
        in_specs=[smem] + [vmem] * 5 + [anywhere] * 5,
        out_specs=vmem,
        scratch_shapes=[
            pltpu.VMEM((4, LEN, KVH * HD), BF),
            pltpu.VMEM((4, LEN, KVH * HD), BF),
            pltpu.VMEM((512, FEATURES), BF),
            pltpu.VMEM((2, 2 * FEATURES // PIECES, HIDDEN), BF),
            pltpu.VMEM((FEATURES, 2 * HIDDEN), BF),
            pltpu.VMEM((HIDDEN, FEATURES), BF),
            pltpu.VMEM((4, 64, HD), F32),
            pltpu.VMEM((16, 16, HD), F32),
            pltpu.VMEM((16, 16, HD), BF),
            pltpu.VMEM((16, 16, HD), BF),
            pltpu.VMEM((CHUNKS, 16, R, 512), BF),
            pltpu.VMEM((256, 256), BF),
            pltpu.VMEM((256, 256), BF),
            pltpu.VMEM((2, CHUNKS, 16, R, FEATURES), BF),
            pltpu.VMEM((2, CHUNKS, 2, 3, 4, R, HALF), BF),
            pltpu.VMEM((2, CHUNKS, 2, 4, R, HALF), BF),
            pltpu.VMEM((2, CHUNKS, 2, 3, R, HALF), BF),
            pltpu.VMEM((CHUNKS, 4, 4, R, FEATURES), BF),
            pltpu.VMEM((CHUNKS, R, FEATURES), F32),
            pltpu.VMEM((CHUNKS, 16, R, 128), F32),
            pltpu.VMEM((CHUNKS, 7, 2, R, 128), F32),
            pltpu.VMEM((CHUNKS, 16, R, 2 * HIDDEN), BF),
            pltpu.VMEM((CHUNKS, 8, R, 2 * HIDDEN), BF),
            pltpu.VMEM((CHUNKS, 3, 2, R, 2 * HIDDEN), BF),
            pltpu.VMEM((CHUNKS, 16, R, HIDDEN), BF),
            pltpu.SemaphoreType.DMA((SENDS,)),
            pltpu.SemaphoreType.DMA((SENDS,)),
            pltpu.SemaphoreType.DMA((8 + 2 + PIECES,)),
        ],
        compiler_params=pltpu.CompilerParams(
            collective_id=0, has_side_effects=True, vmem_limit_bytes=63 * 2**20,
        ),
        cost_estimate=pl.CostEstimate(
            flops=2 * 6 * 10**9, bytes_accessed=28 * 10**6, transcendentals=2 * 10**6
        ),
    )(
        lengths, queries, new_keys, new_values, residual, norm_gain,
        cache_keys, cache_values, out_weight, gate_up, down_weight,
    )


def solution(mesh):
    placed = (
        P(("sec", "grp", "shard"), None),
        P(("sec", "grp", "shard"), None, None),
        P(("sec", "grp", "shard"), None, None),
        P(("sec", "grp", "shard"), None),
        P(("sec", "grp", "shard"), None),
        P(("sec", "grp", "shard")),
        P("shard", ("sec", "grp")),
        P("shard", ("sec", "grp")),
        P(("sec", "grp")),
        P(("sec", "grp"), None, "shard"),
        P("shard", ("sec", "grp")),
    )
    return jax.shard_map(
        local, mesh=mesh, in_specs=placed, out_specs=P("shard", ("sec", "grp")), check_vma=False
    )
```

time: 381 us -> 129 us (0.34)
  waiting for transfers between devices: 268 us -> 0 us
  Pallas kernels: 0 us -> 127 us
  blocking collectives: 45.6 us -> 0 us
  matrix products: 30.4 us -> 0 us
  local copies, waits for them, and re-layouts: 16.8 us -> 1.57 us
  between operations: 13.2 us -> 0.01 us
  other arithmetic: 5.59 us -> 0 us
    reduce_scatter x2 -> x0, waiting for transfers between devices: 150 us -> none  [the longest x1 76.1 us: local(): lax.psum_scatter(partial_out, 'shard', scatter_dimension=0, tiled=True)]
    pallas_call x0 -> x1, Pallas kernels: none -> 127 us  [local(): pl.pallas_call(kernel, out_shape=jax.ShapeDtypeStruct((32, FEATURES), BF)...]
    psum x1 -> x0, waiting for transfers between devices: 89.1 us -> none  [local(): summed = lax.psum(gate_and_up, ('sec', 'grp'))]
    dot_general x6 -> x0, matrix products: 30.4 us -> none  [the longest x1 13.2 us: local(): jnp.dot(lax.all_gather(normed, 'shard', axis=0, tiled=True), both_weights...]
    all_gather x1 -> x0, waiting for transfers between devices: 29.5 us -> none  [local(): lax.all_gather(normed, 'shard', axis=0, tiled=True)]
    all_gather x1 -> x0, blocking collectives: 17.4 us -> none  [local(): lax.all_gather(head_block, ('sec', 'grp'), axis=0, tiled=True)]
    psum x1 -> x0, blocking collectives: 14.3 us -> none  [local(): square_sum = lax.psum(jnp.sum(stream * stream, axis=1), ('sec', 'grp'))]
    all_to_all x1 -> x0, blocking collectives: 13.9 us -> none  [local(): lax.all_to_all(attn, 'shard', split_axis=1, concat_axis=0, tiled=True)]
  transfers between devices with their start and end apart: 4 -> 0, of which waited for: 4 -> 0; matrix products, arithmetic and copies ran while one was open for 4% -> 0% of each run, Pallas kernels for 0% -> 0%
where the time goes in v1:
time: 129 us
  Pallas kernels  127 us (98%)
  local copies, waits for them, and re-layouts  1.57 us (1%)
    pallas_call x1, Pallas kernels, local(): pl.pallas_call(kernel, out_shape=jax.ShapeDtypeStruct((32, FEATURES), BF)...  127 us

profile of v1, /device:TPU:1, one launch (start us, length us, event | category | flops | bytes accessed | tf_op | source)
XLA Modules:
  0.0 128.9 jit_solution(9242418990267803453)
XLA Ops:
  0.0 127.3 %shard_map.109 = bf16[32,2048]{1,0:T(8,128)(2,1)} custom-call(s32[4]{0:T(128)} %lengths.1, bf16[4,8192]{1,0:T(4,128)(2,1)} %queries.1, bf16[4,512]{1,0:T(4,128)(2,1)} %new_keys.1, bf16[4,512]{1,0:T(4,128)(2,1)} %new_values.1, bf16[32,2048]{1,0:T(8,128)(2,1)} %residual.1, f32[2048]{0:T(1024)} %norm_gain.1, bf16[4,512,512]{2,1,0:T(8,128)(2,1)} %cache_keys.1, ...), custom_call_target="tpu_custom_call" | custom-call | flops 12000000000 | bytes 28000000 | tf_op jit(solution)/shard_map/pallas_call | solution.py:404
  127.3 1.6 %copy.13 = bf16[32,2048]{1,0:T(8,128)(2,1)} copy(bf16[32,2048]{1,0:T(8,128)(2,1)} %shard_map.109) | data formatting | bytes 262144

commit v2 on v1

--- a/solution.py
+++ b/solution.py
@@ -22,19 +22,26 @@
 R = 32 // CHUNKS
 HALF = FEATURES // 2
 TILE = 256
-FIRST = 7 * TILE
 PIECES = 4
-LAG = 0
-
-HALVES = (slice(0, HALF), slice(HALF, FEATURES))
-GROUPS = (slice(0, FIRST), slice(FIRST, 2 * HIDDEN))
+ORDER = (
+    (0, "out3"), (1, "attn"), (0, "mid1"), (1, "out1"), (0, "stream1"), (1, "mid1"), (0, "wide1"),
+    (1, "stream1"), (0, "wide3"), (0, "unweave"), (1, "wide1"), (0, "gate0"), (1, "wide3"),
+    (0, "gate3"), (1, "rows"), (0, "reduce2"), (1, "gate0"), (0, "squares"), (1, "squares"),
+    (0, "hidden"), (1, "hidden"), (0, "down2"), (1, "onward"), (0, "down3"), (1, "down3"),
+    (0, "downmid0"), (1, "downmid0"), (0, "downmid1"), (1, "downmid1"), (0, "downmid3"),
+    (1, "end0"), (0, "end1"), (1, "end2"), (0, "end3"), (1, "end3"),
+)
+
+WIDE = HALF // 2
+SPLIT = tuple((h, slice(h * HALF + q * WIDE, h * HALF + (q + 1) * WIDE)) for q in (0, 1) for h in (0, 1))
+GROUPS = (slice(0, 1024), slice(1024, 1792), slice(1792, 2560), slice(2560, 2 * HIDDEN))
 
 
 def kernel(
-    lengths, queries, new_keys, new_values, residual, norm_gain,
+    lengths, queries, new_keys, new_values, norm_gain, residual,
     cache_keys, cache_values, out_weight, gate_up, down_weight,
     mixed,
-    keys, values, wo, raw, gu, wd, q_rows, att, tiles, arrived, attn, unweave, regroup,
+    keys, values, residual_rows, wo, raw, gu, wd, q_rows, att, tiles, arrived, attn, unweave, regroup,
     part, part_in, slab, slab_in, rows, stream, squares, squares_in,
     gates, gates_core, gates_in, hidden,
     send_sem, recv_sem, local_sem,
@@ -97,15 +104,11 @@
         pl.semaphore_signal(barrier, inc=1, device_id=along_z(d, True), device_id_type=MESH)
     pl.semaphore_signal(barrier, inc=1, device_id=across(), device_id_type=MESH)
 
-    wo_in = fetch(out_weight, wo)
     woven = gate_up.reshape(2 * FEATURES, HIDDEN)
     depth = 2 * FEATURES // PIECES
 
     def fetch_raw(p):
         return fetch(woven.at[pl.ds(p * depth, depth), :], raw.at[p % 2])
-
-    raw_in = {0: fetch_raw(0), 1: fetch_raw(1)}
-    wd_in = fetch(down_weight, wd)
 
     i = lax.broadcasted_iota(jnp.int32, (256, 256), 0)
     j = lax.broadcasted_iota(jnp.int32, (256, 256), 1)
@@ -130,6 +133,8 @@
         lax.fori_loop(0, depth // 256, body, 0)
         if p + 2 < PIECES:
             raw_in[p + 2] = fetch_raw(p + 2)
+        if p + 3 == PIECES:
+            raw_in[PIECES] = fetch(down_weight, wd)
 
     scaling = HD ** (-0.5)
     for h in range(KVH * 16):
@@ -138,30 +143,41 @@
     own_values = new_values[...].astype(F32)
     slots = lax.broadcasted_iota(jnp.int32, (1, LEN), 1)
     for r in range(4):
+        usable = slots < lengths[r]
         cache[r][0].wait()
-        cache[r][1].wait()
-        usable = slots < lengths[r]
+        scores, own, own_value = [], [], []
         for k in range(KVH):
             of_head = slice(k * HD, (k + 1) * HD)
             query = q_rows[r, k * 16:(k + 1) * 16, :]
-            scores = lax.dot_general(
+            scores.append(lax.dot_general(
                 query.astype(BF), keys[r, :, of_head], (((1,), (1,)), ((), ())),
                 preferred_element_type=F32,
-            ) * scaling
-            own = jnp.sum(query * own_keys[r:r + 1, of_head], axis=1, keepdims=True) * scaling
-            scores = jnp.where(usable, scores, -1e30)
-            top = jnp.maximum(jnp.max(scores, axis=1, keepdims=True), own)
-            weights = jnp.exp(scores - top)
-            own_weight = jnp.exp(own - top)
-            total = jnp.sum(weights, axis=1, keepdims=True) + own_weight
-            summed = jnp.dot(
-                weights.astype(BF), values[r, :, of_head], preferred_element_type=F32
-            ) + own_weight.astype(BF).astype(F32) * own_values[r:r + 1, of_head]
-            result = summed / total
-            for g in range(4):
-                att[4 * k + g, 4 * r:4 * r + 4, :] = result[4 * g:4 * g + 4, :]
+            ))
+            own.append(query * own_keys[r:r + 1, of_head])
+            own_value.append(jnp.broadcast_to(own_values[r:r + 1, of_head], (16, HD)))
+        scores = jnp.where(usable, jnp.concatenate(scores, axis=0) * scaling, -1e30)
+        own = jnp.sum(jnp.concatenate(own, axis=0), axis=1, keepdims=True) * scaling
+        top = jnp.maximum(jnp.max(scores, axis=1, keepdims=True), own)
+        weights = jnp.exp(scores - top)
+        own_weight = jnp.exp(own - top)
+        total = jnp.sum(weights, axis=1, keepdims=True) + own_weight
+        weights = weights.astype(BF)
+        cache[r][1].wait()
+        summed = jnp.concatenate([
+            jnp.dot(
+                weights[k * 16:(k + 1) * 16], values[r, :, k * HD:(k + 1) * HD],
+                preferred_element_type=F32,
+            ) for k in range(KVH)
+        ], axis=0)
+        own_low = own_weight.astype(BF).astype(F32)
+        result = (summed + own_low * jnp.concatenate(own_value, axis=0)) / total
+        for g in range(16):
+            att[g, 4 * r:4 * r + 4, :] = result[4 * g:4 * g + 4, :]
     tiles[...] = att[...].astype(BF)
 
+    wo_in = fetch(out_weight, wo)
+    residual_in = fetch(residual, residual_rows)
+    raw_in = {0: fetch_raw(0), 1: fetch_raw(1)}
     pl.semaphore_wait(barrier, 22)
 
     exchange = []
@@ -179,16 +195,14 @@
         of_head = grouped[h * 64:(h + 1) * 64, :].reshape(2, CHUNKS, R, HD)
         for c in range(CHUNKS):
             attn[c, pl.ds(2 * block, 2), :, h * HD:(h + 1) * HD] = of_head[:, c]
-    gather = []
-    mine = attn.at[:, pl.ds(2 * block, 2)]
-    for d in (2, 1, 3):
-        gather.append(send(mine, mine, along_z(d)))
-        gather.append(send(mine, mine, along_z(d, True)))
-    gather.append(send(mine, mine, across()))
+    spreads = []
+    for c in range(CHUNKS):
+        mine = attn.at[c, pl.ds(2 * block, 2)]
+        spreads.append([send(mine, mine, along_z(d)) for d in (1, 3, 2)])
+        spreads[c].append(send(mine, mine, across()))
     unweave_piece(1)
     wo_in.wait()
-    for copy in gather:
-        copy.wait_recv()
+    residual_in.wait()
 
     gain = norm_gain[...].reshape(1, FEATURES)
     unscale = 1.0 / (gain * gain)
@@ -208,73 +222,117 @@
 
         lax.fori_loop(0, count, body, 0)
 
-    def scatter_out(u, c, h):
+    def scatter_out(u, c, p):
+        h, cols = SPLIT[p]
         copies = []
         grid = part.at[u, c].reshape(4, 4, R, FEATURES)
         for n, d in enumerate((2, 1, 3)):
             if h == 0:
-                src, to = grid.at[(x + d) % 4, :, :, HALVES[h]], along_x(d)
+                src, to = grid.at[(x + d) % 4, :, :, cols], along_x(d)
             else:
-                src, to = grid.at[:, (y + d) % 4, :, HALVES[h]], along_y(d)
-            copies.append(send(src, part_in.at[u, c, h, n], to))
+                src, to = grid.at[:, (y + d) % 4, :, cols], along_y(d)
+            copies.append(send(src, part_in.at[u, c, p, n], to))
         return copies
 
-    def scatter_mid(u, c, h, copies):
+    def scatter_mid(u, c, p, copies):
+        h, cols = SPLIT[p]
         for copy in copies:
             copy.wait_recv()
         grid = part.at[u, c].reshape(4, 4, R, FEATURES)
-        total = (grid[x, :, :, HALVES[h]] if h == 0 else grid[:, y, :, HALVES[h]]).astype(F32)
+        total = (grid[x, :, :, cols] if h == 0 else grid[:, y, :, cols]).astype(F32)
         for n in range(3):
-            total = total + part_in[u, c, h, n].astype(F32)
-        slab[u, c, h] = total.astype(BF)
+            total = total + part_in[u, c, p, n].astype(F32)
+        slab[u, c, p] = total.astype(BF)
         out = []
         for n, d in enumerate((2, 1, 3)):
             if h == 0:
-                src, to = slab.at[u, c, h, (y + d) % 4], along_y(d)
+                src, to = slab.at[u, c, p, (y + d) % 4], along_y(d)
             else:
-                src, to = slab.at[u, c, h, (x + d) % 4], along_x(d)
-            out.append(send(src, slab_in.at[u, c, h, n], to))
+                src, to = slab.at[u, c, p, (x + d) % 4], along_x(d)
+            out.append(send(src, slab_in.at[u, c, p, n], to))
         return out
 
-    def scatter_end(u, c, h, copies):
+    def scatter_end(u, c, p, copies):
         for copy in copies:
             copy.wait_recv()
-        total = slab[u, c, h, y if h == 0 else x].astype(F32)
+        total = slab[u, c, p, y if SPLIT[p][0] == 0 else x].astype(F32)
         for n in range(3):
-            total = total + slab_in[u, c, h, n].astype(F32)
+            total = total + slab_in[u, c, p, n].astype(F32)
         return total
 
     def chain(c):
+        over = [spreads[c].pop()]
+        for d, copy in zip((1, 3, 2), spreads[c]):
+            copy.wait_recv()
+            from_z = (z - d + 4) % 4
+            there = attn.at[c, pl.ds(2 * ((from_z % 2) * 4 + (from_z // 2) * 2 + core), 2)]
+            over.append(send(there, there, across()))
+        yield "attn"
+        for copy in over:
+            copy.wait_recv()
         lhs = attn.at[c]
         first = []
-        for h in (0, 1):
-            product(c, lhs, wo, HALVES[h], part.at[0])
-            first.append(scatter_out(0, c, h))
-            yield
+        for p, (h, cols) in enumerate(SPLIT):
+            product(c, lhs, wo, cols, part.at[0])
+            first.append(scatter_out(0, c, p))
+            yield f"out{p}"
         second = []
-        for h in (0, 1):
-            second.append(scatter_mid(0, c, h, first[h]))
-            yield
+        for p in range(4):
+            second.append(scatter_mid(0, c, p, first[p]))
+            yield f"mid{p}"
         gathers = []
-        for h in (0, 1):
-            cols = HALVES[h]
-            value = residual[c * R:(c + 1) * R, cols].astype(F32) + scatter_end(0, c, h, second[h])
+        for p, (h, cols) in enumerate(SPLIT):
+            value = residual_rows[c * R:(c + 1) * R, cols].astype(F32) + scatter_end(0, c, p, second[p])
             stream[c, :, cols] = value
             rows[c, x, y, :, cols] = (value * gain[:, cols]).astype(BF)
             here = rows.at[c, x, y, :, cols]
             gathers.append([
                 send(here, here, along_y(d) if h == 0 else along_x(d)) for d in (2, 1, 3)
             ])
-        yield
+            yield f"stream{p}"
         wider = []
-        for h in (0, 1):
-            for copy in gathers[h]:
+        for p, (h, cols) in enumerate(SPLIT):
+            for copy in gathers[p]:
                 copy.wait_recv()
-            here = rows.at[c, x, :, :, HALVES[h]] if h == 0 else rows.at[c, :, y, :, HALVES[h]]
+            here = rows.at[c, x, :, :, cols] if h == 0 else rows.at[c, :, y, :, cols]
             wider += [send(here, here, along_x(d) if h == 0 else along_y(d)) for d in (2, 1, 3)]
-            yield
+            yield f"wide{p}"
         for copy in wider:
             copy.wait_recv()
+        yield "rows"
+
+        lhs = rows.at[c].reshape(16, R, FEATURES)
+        crossing = []
+        reduced = []
+        theirs = pl.ds(8 * (1 - core), 8)
+
+        def cross(g):
+            product(c, lhs, gu, GROUPS[g], gates)
+            crossing.append(send(
+                gates.at[c, theirs, :, GROUPS[g]], gates_core.at[c, :, :, GROUPS[g]], across()
+            ))
+
+        def reduce(g):
+            crossing[g].wait_recv()
+            for n, d in enumerate((2, 1, 3)):
+                to = (z + d) % 4
+                at = pl.ds(8 * core + 2 * to, 2)
+                gates[c, at, :, GROUPS[g]] = (
+                    gates[c, at, :, GROUPS[g]].astype(F32)
+                    + gates_core[c, pl.ds(2 * to, 2), :, GROUPS[g]].astype(F32)
+                ).astype(BF)
+                reduced.append(send(
+                    gates.at[c, at, :, GROUPS[g]], gates_in.at[c, n, :, :, GROUPS[g]], along_z(d)
+                ))
+
+        cross(0)
+        yield "gate0"
+        for g in range(1, len(GROUPS)):
+            cross(g)
+            yield f"gate{g}"
+            reduce(g - 1)
+            yield f"reduce{g - 1}"
+        reduce(len(GROUPS) - 1)
 
         def square(b, carry):
             v = rows[c, b // 4, b % 4].astype(F32)
@@ -295,30 +353,7 @@
                     across() if d == 0 else along_z(d, other),
                 ))
                 n += 1
-        yield
-        lhs = rows.at[c].reshape(16, R, FEATURES)
-        crossing = []
-        theirs = pl.ds(8 * (1 - core), 8)
-        for g in (0, 1):
-            product(c, lhs, gu, GROUPS[g], gates)
-            crossing.append(send(
-                gates.at[c, theirs, :, GROUPS[g]], gates_core.at[c, :, :, GROUPS[g]], across()
-            ))
-            yield
-        reduced = []
-        for g in (0, 1):
-            crossing[g].wait_recv()
-            for n, d in enumerate((2, 1, 3)):
-                to = (z + d) % 4
-                at = pl.ds(8 * core + 2 * to, 2)
-                gates[c, at, :, GROUPS[g]] = (
-                    gates[c, at, :, GROUPS[g]].astype(F32)
-                    + gates_core[c, pl.ds(2 * to, 2), :, GROUPS[g]].astype(F32)
-                ).astype(BF)
-                reduced.append(send(
-                    gates.at[c, at, :, GROUPS[g]], gates_in.at[c, n, :, :, GROUPS[g]], along_z(d)
-                ))
-            yield
+        yield "squares"
         for copy in square_copies + reduced:
             copy.wait_recv()
         owner = 2 * (4 * core + z)
@@ -340,58 +375,45 @@
         here = hidden.at[c, pl.ds(owner, 2)]
         spread = [send(here, here, along_z(d)) for d in (2, 1, 3)]
         over = [send(here, here, across())]
-        yield
-        for d, copy in sorted(zip((2, 1, 3), spread), key=lambda e: e[0] == 2):
+        yield "hidden"
+        for d, copy in ((1, spread[1]), (3, spread[2]), (2, spread[0])):
             copy.wait_recv()
             there = hidden.at[c, pl.ds(2 * (4 * core + (z - d + 4) % 4), 2)]
             over.append(send(there, there, across()))
-        yield
+            if d != 1:
+                yield "onward" if d == 3 else "over"
         for copy in over:
             copy.wait_recv()
         lhs = hidden.at[c]
         first = []
-        for h in (0, 1):
-            product(c, lhs, wd, HALVES[h], part.at[1])
-            first.append(scatter_out(1, c, h))
-            yield
+        for p, (h, cols) in enumerate(SPLIT):
+            product(c, lhs, wd, cols, part.at[1])
+            first.append(scatter_out(1, c, p))
+            yield f"down{p}"
         second = []
-        for h in (0, 1):
-            second.append(scatter_mid(1, c, h, first[h]))
-            yield
-        for h in (0, 1):
-            cols = HALVES[h]
+        for p in range(4):
+            second.append(scatter_mid(1, c, p, first[p]))
+            yield f"downmid{p}"
+        for p, (h, cols) in enumerate(SPLIT):
             mixed[c * R:(c + 1) * R, cols] = (
-                stream[c, :, cols] + scatter_end(1, c, h, second[h])
+                stream[c, :, cols] + scatter_end(1, c, p, second[p])
             ).astype(BF)
+            yield f"end{p}"
 
     chains = [chain(c) for c in range(CHUNKS)]
-    done = [0] * CHUNKS
-    live = [True] * CHUNKS
-    rest = [lambda: unweave_piece(2), lambda: unweave_piece(3)]
-
-    def advance(c):
-        if live[c]:
-            try:
-                next(chains[c])
-                done[c] += 1
-            except StopIteration:
-                live[c] = False
-
-    turn = 0
-    while any(live):
-        for c in range(CHUNKS):
-            if turn >= c * LAG:
-                advance(c)
-        turn += 1
-        if turn == 2:
-            for piece in rest:
-                piece()
-            wd_in.wait()
+    for c, last in ORDER:
+        if last == "unweave":
+            unweave_piece(2)
+            unweave_piece(3)
+            raw_in[PIECES].wait()
+            continue
+        while next(chains[c]) != last:
+            pass
     for copy in sent:
         copy.wait_send()
 
 
-SENDS = 15 + 7 + CHUNKS * (6 + 6 + 6 + 6 + 7 + 2 + 6 + 3 + 4 + 6 + 6)
+SENDS = 15 + CHUNKS * (7 + 6 * 12 + 7 + 16 + 7)
 
 
 def local(
@@ -404,11 +426,12 @@
     return pl.pallas_call(
         kernel,
         out_shape=jax.ShapeDtypeStruct((32, FEATURES), BF),
-        in_specs=[smem] + [vmem] * 5 + [anywhere] * 5,
+        in_specs=[smem] + [vmem] * 4 + [anywhere] * 6,
         out_specs=vmem,
         scratch_shapes=[
             pltpu.VMEM((4, LEN, KVH * HD), BF),
             pltpu.VMEM((4, LEN, KVH * HD), BF),
+            pltpu.VMEM((32, FEATURES), BF),
             pltpu.VMEM((512, FEATURES), BF),
             pltpu.VMEM((2, 2 * FEATURES // PIECES, HIDDEN), BF),
             pltpu.VMEM((FEATURES, 2 * HIDDEN), BF),
@@ -421,9 +444,9 @@
             pltpu.VMEM((256, 256), BF),
             pltpu.VMEM((256, 256), BF),
             pltpu.VMEM((2, CHUNKS, 16, R, FEATURES), BF),
-            pltpu.VMEM((2, CHUNKS, 2, 3, 4, R, HALF), BF),
-            pltpu.VMEM((2, CHUNKS, 2, 4, R, HALF), BF),
-            pltpu.VMEM((2, CHUNKS, 2, 3, R, HALF), BF),
+            pltpu.VMEM((2, CHUNKS, 4, 3, 4, R, WIDE), BF),
+            pltpu.VMEM((2, CHUNKS, 4, 4, R, WIDE), BF),
+            pltpu.VMEM((2, CHUNKS, 4, 3, R, WIDE), BF),
             pltpu.VMEM((CHUNKS, 4, 4, R, FEATURES), BF),
             pltpu.VMEM((CHUNKS, R, FEATURES), F32),
             pltpu.VMEM((CHUNKS, 16, R, 128), F32),
@@ -434,7 +457,7 @@
             pltpu.VMEM((CHUNKS, 16, R, HIDDEN), BF),
             pltpu.SemaphoreType.DMA((SENDS,)),
             pltpu.SemaphoreType.DMA((SENDS,)),
-            pltpu.SemaphoreType.DMA((8 + 2 + PIECES,)),
+            pltpu.SemaphoreType.DMA((8 + 3 + PIECES,)),
         ],
         compiler_params=pltpu.CompilerParams(
             collective_id=0, has_side_effects=True, vmem_limit_bytes=63 * 2**20,
@@ -443,7 +466,7 @@
             flops=2 * 6 * 10**9, bytes_accessed=28 * 10**6, transcendentals=2 * 10**6
         ),
     )(
-        lengths, queries, new_keys, new_values, residual, norm_gain,
+        lengths, queries, new_keys, new_values, norm_gain, residual,
         cache_keys, cache_values, out_weight, gate_up, down_weight,
     )
 

time: 129 us -> 103 us (0.80)
  Pallas kernels: 127 us -> 101 us
    pallas_call x1, Pallas kernels: 127 us -> 101 us  [local(): pl.pallas_call(kernel, out_shape=jax.ShapeDtypeStruct((32, FEATURES), BF)...]
where the time goes in v2:
time: 103 us
  Pallas kernels  101 us (98%)
  local copies, waits for them, and re-layouts  1.57 us (2%)
    pallas_call x1, Pallas kernels, local(): pl.pallas_call(kernel, out_shape=jax.ShapeDtypeStruct((32, FEATURES), BF)...  101 us

profile of v2, /device:TPU:1, one launch (start us, length us, event | category | flops | bytes accessed | tf_op | source)
XLA Modules:
  0.0 102.8 jit_solution(14687509574359428770)
XLA Ops:
  0.0 101.3 %shard_map.109 = bf16[32,2048]{1,0:T(8,128)(2,1)} custom-call(s32[4]{0:T(128)} %lengths.1, bf16[4,8192]{1,0:T(4,128)(2,1)} %queries.1, bf16[4,512]{1,0:T(4,128)(2,1)} %new_keys.1, bf16[4,512]{1,0:T(4,128)(2,1)} %new_values.1, f32[2048]{0:T(1024)} %norm_gain.1, bf16[32,2048]{1,0:T(8,128)(2,1)} %residual.1, bf16[4,512,512]{2,1,0:T(8,128)(2,1)} %cache_keys.1, ...), custom_call_target="tpu_custom_call" | custom-call | flops 12000000000 | bytes 28000000 | tf_op jit(solution)/shard_map/pallas_call | solution.py:426
  101.3 1.6 %copy.13 = bf16[32,2048]{1,0:T(8,128)(2,1)} copy(bf16[32,2048]{1,0:T(8,128)(2,1)} %shard_map.109) | data formatting | bytes 262144

commit v3 on v2

--- a/solution.py
+++ b/solution.py
@@ -73,16 +73,24 @@
         return {"grp": (grp // 2) * 2 + (1 - core)}
 
     sent = []
-
-    def send(src, dst, to):
-        i = len(sent)
+    groups = []
+
+    def group():
+        groups.append(len(groups))
+        return groups[-1]
+
+    def send(src, dst, to, i=None):
+        i = group() if i is None else i
         copy = pltpu.make_async_remote_copy(
-            src_ref=src, dst_ref=dst, send_sem=send_sem.at[i], recv_sem=recv_sem.at[i],
-            device_id=to, device_id_type=MESH,
+            src_ref=src, dst_ref=dst, send_sem=send_sem.at[len(sent) % SEND_SEMS],
+            recv_sem=recv_sem.at[i], device_id=to, device_id_type=MESH,
         )
         copy.start()
         sent.append(copy)
         return copy
+
+    def settle(ref, i):
+        pltpu.make_async_copy(ref, ref, recv_sem.at[i]).wait()
 
     fetched = []
 
@@ -109,13 +117,6 @@
 
     def fetch_raw(p):
         return fetch(woven.at[pl.ds(p * depth, depth), :], raw.at[p % 2])
-
-    i = lax.broadcasted_iota(jnp.int32, (256, 256), 0)
-    j = lax.broadcasted_iota(jnp.int32, (256, 256), 1)
-    unweave[...] = jnp.where(j == (i % 128) * 2 + i // 128, 1.0, 0.0).astype(BF)
-    regroup[...] = jnp.where(
-        j == ((i % 64) // 4) * 16 + (i % 4) * 4 + i // 64, 1.0, 0.0
-    ).astype(BF)
 
     def unweave_piece(p):
         raw_in[p].wait()
@@ -180,14 +181,19 @@
     raw_in = {0: fetch_raw(0), 1: fetch_raw(1)}
     pl.semaphore_wait(barrier, 22)
 
-    exchange = []
+    exchange = group()
     for d in range(1, 16):
         to = (shard + d) % 16
-        exchange.append(send(tiles.at[to], arrived.at[shard], plane(to)))
+        send(tiles.at[to], arrived.at[shard], plane(to), exchange)
     arrived[shard] = tiles[shard]
+    i = lax.broadcasted_iota(jnp.int32, (256, 256), 0)
+    j = lax.broadcasted_iota(jnp.int32, (256, 256), 1)
+    regroup[...] = jnp.where(
+        j == ((i & 60) << 2) + ((i & 3) << 2) + (i >> 6), 1.0, 0.0
+    ).astype(BF)
+    unweave[...] = jnp.where(j == ((i & 127) << 1) + (i >> 7), 1.0, 0.0).astype(BF)
     unweave_piece(0)
-    for copy in exchange:
-        copy.wait_recv()
+    settle(arrived.at[pl.ds(0, 15)], exchange)
     grouped = jnp.dot(
         regroup[...], arrived[...].reshape(256, HD), preferred_element_type=F32
     ).astype(BF)
@@ -199,7 +205,8 @@
     for c in range(CHUNKS):
         mine = attn.at[c, pl.ds(2 * block, 2)]
         spreads.append([send(mine, mine, along_z(d)) for d in (1, 3, 2)])
-        spreads[c].append(send(mine, mine, across()))
+        spreads[c].append(group())
+        send(mine, mine, across(), spreads[c][-1])
     unweave_piece(1)
     wo_in.wait()
     residual_in.wait()
@@ -224,52 +231,49 @@
 
     def scatter_out(u, c, p):
         h, cols = SPLIT[p]
-        copies = []
+        i = group()
         grid = part.at[u, c].reshape(4, 4, R, FEATURES)
         for n, d in enumerate((2, 1, 3)):
             if h == 0:
                 src, to = grid.at[(x + d) % 4, :, :, cols], along_x(d)
             else:
                 src, to = grid.at[:, (y + d) % 4, :, cols], along_y(d)
-            copies.append(send(src, part_in.at[u, c, p, n], to))
-        return copies
-
-    def scatter_mid(u, c, p, copies):
+            send(src, part_in.at[u, c, p, n], to, i)
+        return i
+
+    def scatter_mid(u, c, p, i):
         h, cols = SPLIT[p]
-        for copy in copies:
-            copy.wait_recv()
+        settle(part_in.at[u, c, p], i)
         grid = part.at[u, c].reshape(4, 4, R, FEATURES)
         total = (grid[x, :, :, cols] if h == 0 else grid[:, y, :, cols]).astype(F32)
         for n in range(3):
             total = total + part_in[u, c, p, n].astype(F32)
         slab[u, c, p] = total.astype(BF)
-        out = []
+        i = group()
         for n, d in enumerate((2, 1, 3)):
             if h == 0:
                 src, to = slab.at[u, c, p, (y + d) % 4], along_y(d)
             else:
                 src, to = slab.at[u, c, p, (x + d) % 4], along_x(d)
-            out.append(send(src, slab_in.at[u, c, p, n], to))
-        return out
-
-    def scatter_end(u, c, p, copies):
-        for copy in copies:
-            copy.wait_recv()
+            send(src, slab_in.at[u, c, p, n], to, i)
+        return i
+
+    def scatter_end(u, c, p, i):
+        settle(slab_in.at[u, c, p], i)
         total = slab[u, c, p, y if SPLIT[p][0] == 0 else x].astype(F32)
         for n in range(3):
             total = total + slab_in[u, c, p, n].astype(F32)
         return total
 
     def chain(c):
-        over = [spreads[c].pop()]
+        over = spreads[c].pop()
         for d, copy in zip((1, 3, 2), spreads[c]):
             copy.wait_recv()
             from_z = (z - d + 4) % 4
             there = attn.at[c, pl.ds(2 * ((from_z % 2) * 4 + (from_z // 2) * 2 + core), 2)]
-            over.append(send(there, there, across()))
+            send(there, there, across(), over)
         yield "attn"
-        for copy in over:
-            copy.wait_recv()
+        settle(attn.at[c, pl.ds(0, 8)], over)
         lhs = attn.at[c]
         first = []
         for p, (h, cols) in enumerate(SPLIT):
@@ -286,24 +290,23 @@
             stream[c, :, cols] = value
             rows[c, x, y, :, cols] = (value * gain[:, cols]).astype(BF)
             here = rows.at[c, x, y, :, cols]
-            gathers.append([
-                send(here, here, along_y(d) if h == 0 else along_x(d)) for d in (2, 1, 3)
-            ])
+            gathers.append(group())
+            for d in (2, 1, 3):
+                send(here, here, along_y(d) if h == 0 else along_x(d), gathers[p])
             yield f"stream{p}"
-        wider = []
+        wider = group()
         for p, (h, cols) in enumerate(SPLIT):
-            for copy in gathers[p]:
-                copy.wait_recv()
+            settle(rows.at[c, 0, pl.ds(0, 3), :, cols], gathers[p])
             here = rows.at[c, x, :, :, cols] if h == 0 else rows.at[c, :, y, :, cols]
-            wider += [send(here, here, along_x(d) if h == 0 else along_y(d)) for d in (2, 1, 3)]
+            for d in (2, 1, 3):
+                send(here, here, along_x(d) if h == 0 else along_y(d), wider)
             yield f"wide{p}"
-        for copy in wider:
-            copy.wait_recv()
+        settle(rows.at[c, pl.ds(0, 3)], wider)
         yield "rows"
 
         lhs = rows.at[c].reshape(16, R, FEATURES)
         crossing = []
-        reduced = []
+        reduced = group()
         theirs = pl.ds(8 * (1 - core), 8)
 
         def cross(g):
@@ -321,9 +324,9 @@
                     gates[c, at, :, GROUPS[g]].astype(F32)
                     + gates_core[c, pl.ds(2 * to, 2), :, GROUPS[g]].astype(F32)
                 ).astype(BF)
-                reduced.append(send(
-                    gates.at[c, at, :, GROUPS[g]], gates_in.at[c, n, :, :, GROUPS[g]], along_z(d)
-                ))
+                send(
+                    gates.at[c, at, :, GROUPS[g]], gates_in.at[c, n, :, :, GROUPS[g]], along_z(d), reduced
+                )
 
         cross(0)
         yield "gate0"
@@ -341,21 +344,21 @@
             return carry
 
         lax.fori_loop(0, 16, square, 0)
-        square_copies = []
+        squared = group()
         n = 0
         for other in (False, True):
             for d in (0, 1, 2, 3):
                 if d == 0 and not other:
                     continue
                 owner = (1 - core if other else core) * 4 + (z + d) % 4
-                square_copies.append(send(
+                send(
                     squares.at[c, pl.ds(2 * owner, 2)], squares_in.at[c, n],
-                    across() if d == 0 else along_z(d, other),
-                ))
+                    across() if d == 0 else along_z(d, other), squared,
+                )
                 n += 1
         yield "squares"
-        for copy in square_copies + reduced:
-            copy.wait_recv()
+        settle(squares_in.at[c], squared)
+        settle(gates_in.at[c], reduced)
         owner = 2 * (4 * core + z)
         total = squares[c, pl.ds(owner, 2)]
         for n in range(7):
@@ -374,16 +377,16 @@
         hidden[c, pl.ds(owner, 2)] = (gate / (1.0 + jnp.exp(-gate)) * up).astype(BF)
         here = hidden.at[c, pl.ds(owner, 2)]
         spread = [send(here, here, along_z(d)) for d in (2, 1, 3)]
-        over = [send(here, here, across())]
+        over = group()
+        send(here, here, across(), over)
         yield "hidden"
         for d, copy in ((1, spread[1]), (3, spread[2]), (2, spread[0])):
             copy.wait_recv()
             there = hidden.at[c, pl.ds(2 * (4 * core + (z - d + 4) % 4), 2)]
-            over.append(send(there, there, across()))
+            send(there, there, across(), over)
             if d != 1:
                 yield "onward" if d == 3 else "over"
-        for copy in over:
-            copy.wait_recv()
+        settle(hidden.at[c, pl.ds(0, 8)], over)
         lhs = hidden.at[c]
         first = []
         for p, (h, cols) in enumerate(SPLIT):
@@ -409,11 +412,13 @@
             continue
         while next(chains[c]) != last:
             pass
+    assert len(groups) == RECV_SEMS
     for copy in sent:
         copy.wait_send()
 
 
-SENDS = 15 + CHUNKS * (7 + 6 * 12 + 7 + 16 + 7)
+SEND_SEMS = 8
+RECV_SEMS = 1 + CHUNKS * 35
 
 
 def local(
@@ -455,8 +460,8 @@
             pltpu.VMEM((CHUNKS, 8, R, 2 * HIDDEN), BF),
             pltpu.VMEM((CHUNKS, 3, 2, R, 2 * HIDDEN), BF),
             pltpu.VMEM((CHUNKS, 16, R, HIDDEN), BF),
-            pltpu.SemaphoreType.DMA((SENDS,)),
-            pltpu.SemaphoreType.DMA((SENDS,)),
+            pltpu.SemaphoreType.DMA((SEND_SEMS,)),
+            pltpu.SemaphoreType.DMA((RECV_SEMS,)),
             pltpu.SemaphoreType.DMA((8 + 3 + PIECES,)),
         ],
         compiler_params=pltpu.CompilerParams(

time: 103 us -> 99.4 us (0.965)
  Pallas kernels: 101 us -> 97.7 us
    pallas_call x1, Pallas kernels: 101 us -> 97.7 us  [local(): pl.pallas_call(kernel, out_shape=jax.ShapeDtypeStruct((32, FEATURES), BF)...]
where the time goes in v3:
time: 99.4 us; the launch traced here: 99.3 us
  Pallas kernels  97.7 us (98%)
  local copies, waits for them, and re-layouts  1.57 us (2%)
    pallas_call x1, Pallas kernels, local(): pl.pallas_call(kernel, out_shape=jax.ShapeDtypeStruct((32, FEATURES), BF)...  97.7 us

profile of v3, /device:TPU:1, one launch (start us, length us, event | category | flops | bytes accessed | tf_op | source)
XLA Modules:
  0.0 99.3 jit_solution(7845617825320502396)
XLA Ops:
  0.0 97.7 %shard_map.109 = bf16[32,2048]{1,0:T(8,128)(2,1)} custom-call(s32[4]{0:T(128)} %lengths.1, bf16[4,8192]{1,0:T(4,128)(2,1)} %queries.1, bf16[4,512]{1,0:T(4,128)(2,1)} %new_keys.1, bf16[4,512]{1,0:T(4,128)(2,1)} %new_values.1, f32[2048]{0:T(1024)} %norm_gain.1, bf16[32,2048]{1,0:T(8,128)(2,1)} %residual.1, bf16[4,512,512]{2,1,0:T(8,128)(2,1)} %cache_keys.1, ...), custom_call_target="tpu_custom_call" | custom-call | flops 12000000000 | bytes 28000000 | tf_op jit(solution)/shard_map/pallas_call | solution.py:431
  97.7 1.6 %copy.13 = bf16[32,2048]{1,0:T(8,128)(2,1)} copy(bf16[32,2048]{1,0:T(8,128)(2,1)} %shard_map.109) | data formatting | bytes 262144

commit v4 on v3

--- a/solution.py
+++ b/solution.py
@@ -24,17 +24,21 @@
 TILE = 256
 PIECES = 4
 ORDER = (
-    (0, "out3"), (1, "attn"), (0, "mid1"), (1, "out1"), (0, "stream1"), (1, "mid1"), (0, "wide1"),
-    (1, "stream1"), (0, "wide3"), (0, "unweave"), (1, "wide1"), (0, "gate0"), (1, "wide3"),
-    (0, "gate3"), (1, "rows"), (0, "reduce2"), (1, "gate0"), (0, "squares"), (1, "squares"),
-    (0, "hidden"), (1, "hidden"), (0, "down2"), (1, "onward"), (0, "down3"), (1, "down3"),
-    (0, "downmid0"), (1, "downmid0"), (0, "downmid1"), (1, "downmid1"), (0, "downmid3"),
-    (1, "end0"), (0, "end1"), (1, "end2"), (0, "end3"), (1, "end3"),
+    (0, "out7"), (1, "attn"), (0, "unweave"), (1, "out0"), (0, "mid0"), (1, "out1"), (0, "mid4"),
+    (1, "out2"), (0, "mid5"), (1, "out3"), (0, "mid7"), (1, "out4"), (0, "stream0"), (1, "out5"),
+    (0, "stream3"), (1, "out7"), (0, "stream4"), (1, "mid2"), (0, "stream6"), (1, "mid3"),
+    (0, "stream7"), (1, "mid5"), (0, "wide3"), (1, "mid7"), (0, "wide4"), (1, "stream4"),
+    (0, "wide5"), (1, "stream5"), (0, "wide7"), (1, "wide5"), (0, "gate0"), (1, "wide6"),
+    (0, "gate2"), (1, "wide7"), (0, "reduce3"), (1, "gate0"), (0, "squares"), (1, "squares"),
+    (0, "hidden"), (1, "hidden"), (0, "down4"), (1, "onward"), (0, "down6"), (1, "over"),
+    (0, "down7"), (1, "down7"), (0, "downmid0"), (1, "downmid2"), (0, "downmid4"), (1, "downmid5"),
+    (0, "downmid7"), (1, "downmid7"), (0, "end0"), (1, "end1"), (0, "end1"), (1, "end2"),
+    (0, "end3"), (1, "end3"), (0, "end5"), (1, "end5"), (0, "end7"), (1, "end7"),
 )
 
-WIDE = HALF // 2
-SPLIT = tuple((h, slice(h * HALF + q * WIDE, h * HALF + (q + 1) * WIDE)) for q in (0, 1) for h in (0, 1))
-GROUPS = (slice(0, 1024), slice(1024, 1792), slice(1792, 2560), slice(2560, 2 * HIDDEN))
+WIDE = HALF // 4
+SPLIT = tuple((h, slice(h * HALF + q * WIDE, h * HALF + (q + 1) * WIDE)) for q in range(4) for h in (0, 1))
+GROUPS = tuple(slice(a, b) for a, b in zip((0, 512, 1024, 1792, 2560), (512, 1024, 1792, 2560, 3328)))
 
 
 def kernel(
@@ -281,7 +285,7 @@
             first.append(scatter_out(0, c, p))
             yield f"out{p}"
         second = []
-        for p in range(4):
+        for p in range(len(SPLIT)):
             second.append(scatter_mid(0, c, p, first[p]))
             yield f"mid{p}"
         gathers = []
@@ -394,7 +398,7 @@
             first.append(scatter_out(1, c, p))
             yield f"down{p}"
         second = []
-        for p in range(4):
+        for p in range(len(SPLIT)):
             second.append(scatter_mid(1, c, p, first[p]))
             yield f"downmid{p}"
         for p, (h, cols) in enumerate(SPLIT):
@@ -418,7 +422,7 @@
 
 
 SEND_SEMS = 8
-RECV_SEMS = 1 + CHUNKS * 35
+RECV_SEMS = 1 + CHUNKS * (11 + 5 * len(SPLIT) + len(GROUPS))
 
 
 def local(
@@ -449,9 +453,9 @@
             pltpu.VMEM((256, 256), BF),
             pltpu.VMEM((256, 256), BF),
             pltpu.VMEM((2, CHUNKS, 16, R, FEATURES), BF),
-            pltpu.VMEM((2, CHUNKS, 4, 3, 4, R, WIDE), BF),
-            pltpu.VMEM((2, CHUNKS, 4, 4, R, WIDE), BF),
-            pltpu.VMEM((2, CHUNKS, 4, 3, R, WIDE), BF),
+            pltpu.VMEM((2, CHUNKS, len(SPLIT), 3, 4, R, WIDE), BF),
+            pltpu.VMEM((2, CHUNKS, len(SPLIT), 4, R, WIDE), BF),
+            pltpu.VMEM((2, CHUNKS, len(SPLIT), 3, R, WIDE), BF),
             pltpu.VMEM((CHUNKS, 4, 4, R, FEATURES), BF),
             pltpu.VMEM((CHUNKS, R, FEATURES), F32),
             pltpu.VMEM((CHUNKS, 16, R, 128), F32),

time: 99.4 us -> 98.1 us (0.987)
  Pallas kernels: 97.7 us -> 96.3 us
    pallas_call x1, Pallas kernels: 97.7 us -> 96.3 us  [local(): pl.pallas_call(kernel, out_shape=jax.ShapeDtypeStruct((32, FEATURES), BF)...]
where the time goes in v4:
time: 98.1 us; the launch traced here: 97.9 us
  Pallas kernels  96.3 us (98%)
  local copies, waits for them, and re-layouts  1.57 us (2%)
    pallas_call x1, Pallas kernels, local(): pl.pallas_call(kernel, out_shape=jax.ShapeDtypeStruct((32, FEATURES), BF)...  96.3 us

profile of v4, /device:TPU:1, one launch (start us, length us, event | category | flops | bytes accessed | tf_op | source)
XLA Modules:
  0.0 97.9 jit_solution(1668402218718463386)
XLA Ops:
  0.0 96.3 %shard_map.109 = bf16[32,2048]{1,0:T(8,128)(2,1)} custom-call(s32[4]{0:T(128)} %lengths.1, bf16[4,8192]{1,0:T(4,128)(2,1)} %queries.1, bf16[4,512]{1,0:T(4,128)(2,1)} %new_keys.1, bf16[4,512]{1,0:T(4,128)(2,1)} %new_values.1, f32[2048]{0:T(1024)} %norm_gain.1, bf16[32,2048]{1,0:T(8,128)(2,1)} %residual.1, bf16[4,512,512]{2,1,0:T(8,128)(2,1)} %cache_keys.1, ...), custom_call_target="tpu_custom_call" | custom-call | flops 12000000000 | bytes 28000000 | tf_op jit(solution)/shard_map/pallas_call | solution.py:435
  96.3 1.6 %copy.13 = bf16[32,2048]{1,0:T(8,128)(2,1)} copy(bf16[32,2048]{1,0:T(8,128)(2,1)} %shard_map.109) | data formatting | bytes 262144
